TPU v7x, 32 devices: a whole 2x2x4 slice. The times are simulated.
32 devices in a mesh: groups: 2 (over x), ctx: 16 (over z, y, core).
Axes of the slice: x: 2, y: 2, z: 4, core: 2. Of those that a mesh axis runs over, the one named last changes fastest.
Arguments:
- q_raw: bfloat16 [16384, 1024], P(('groups', 'ctx')), parts along dimension 0, may hold values from -6 to 6
- k_raw: bfloat16 [16384, 1024], P(('groups', 'ctx')), parts along dimension 0, may hold values from -6 to 6
- v_raw: bfloat16 [16384, 2048], P(('groups', 'ctx')), parts along dimension 0, may hold values from -6 to 6
- conv_weight: float32 [4, 4096], replicated, may hold values from -3 to 3
- gate_log: float32 [16384, 16], P(('groups', 'ctx')), parts along dimension 0, may hold values from -1 to 0
- beta: float32 [16384, 16], P(('groups', 'ctx')), parts along dimension 0, may hold values from 0 to 0.9
- gate_z: bfloat16 [16384, 2048], P(('groups', 'ctx')), parts along dimension 0, may hold values from -6 to 6
- norm_gain: float32 [128], replicated, may hold values from 0.1 to 1.9
- doc_start: int32 [32], P(('groups', 'ctx')), parts along dimension 0, may hold values from 0 to 512, as said below
Outputs:
- mixed: bfloat16 [16384, 2048], P(('groups', 'ctx')), parts along dimension 0
There are 2 independent parts, one for each index of `groups`. A program takes and returns all parts, laid end to end along the dimension named above; an argument that names none is the same for every part. Nothing has to cross between parts.
Inputs may be any that keep to these rules, and one draw needn't show every extreme that they name: `doc_start`: at most one document begins in a slab; the value is 512 where none begins.
All inputs are finite; a program needn't handle non-finite values.
Results may differ from a plain program's by a relative error of at most 0.0045.
Values may be sent and summed in bfloat16 or wider, within the bound.
A program may use at most 128 MiB of HBM per device.

v0:
```python
import jax
import jax.numpy as jnp
from jax import lax
from jax.sharding import PartitionSpec as P

HK = 8
HV = 16
DK = 128
DV = 128
SPAN = 64


precise = lax.Precision.HIGHEST


def passed_along(x, axis, by):
    count = lax.axis_size(axis)
    pairs = [(i, i + by) for i in range(count) if 0 <= i + by < count]
    return lax.ppermute(x, axis, pairs)


def conv_silu(raw_block, rim_rows, block_docs, rim_docs, weights):
    extended = jnp.concatenate([rim_rows, raw_block], axis=0)
    extended_docs = jnp.concatenate([rim_docs, block_docs], axis=0)
    length = raw_block.shape[0]
    summed = jnp.zeros(raw_block.shape, jnp.float32)
    for offset in range(weights.shape[0]):
        window = extended[offset : offset + length].astype(jnp.float32)
        usable = (extended_docs[offset : offset + length] == block_docs)[:, None]
        summed = summed + jnp.where(usable, weights[offset][None, :] * window, 0.0)
    return jax.nn.silu(summed).astype(jnp.bfloat16)


def unit_rows(values, head_count, factor):
    shaped = values.astype(jnp.float32).reshape(values.shape[0], head_count, -1)
    return shaped / jnp.sqrt(jnp.sum(shaped * shaped, axis=-1, keepdims=True) + 1e-06) * factor


def unit_lower_inverse(lower_part):
    length = lower_part.shape[-1]
    eye_rows = jnp.eye(length, dtype=jnp.float32)[None]
    power = -lower_part
    inverse = eye_rows + power
    for step in range((length - 1).bit_length() - 1):
        power = jnp.einsum("hij,hjk->hik", power, power, precision=precise)
        inverse = jnp.einsum("hij,hjk->hik", inverse, eye_rows + power, precision=precise)
    return inverse


def block_terms(query_conv, key_conv, value_conv, gate_block, beta_block, block_docs, prior_doc):
    length = query_conv.shape[0]
    queries = jnp.repeat(unit_rows(query_conv, HK, DK ** (-0.5)), HV // HK, axis=1)
    key_rows = jnp.repeat(unit_rows(key_conv, HK, 1.0), HV // HK, axis=1)
    values = value_conv.astype(jnp.float32).reshape(length, HV, DV)
    cumulative = jnp.cumsum(gate_block, axis=0)
    places = jnp.arange(length)
    same_doc = block_docs[:, None] == block_docs[None, :]
    within = (places[:, None] >= places[None, :]) & same_doc
    strictly = (places[:, None] > places[None, :]) & same_doc
    heads_first = cumulative.T
    spread_log = heads_first[:, :, None] - heads_first[:, None, :]
    decay_incl = jnp.exp(jnp.where(within[None], spread_log, -jnp.inf))
    decay_strict = jnp.where(strictly[None], decay_incl, 0.0)
    key_gram = jnp.einsum("ihd,jhd->hij", key_rows, key_rows, precision=precise)
    lower_part = beta_block.T[:, :, None] * key_gram * decay_strict
    start_open = (block_docs == prior_doc).astype(jnp.float32)
    end_open = (block_docs == block_docs[-1]).astype(jnp.float32)
    carries = (block_docs[-1] == prior_doc).astype(jnp.float32)
    growth = jnp.exp(cumulative)
    weight_in = (beta_block * growth * start_open[:, None])[:, :, None] * key_rows
    value_in = beta_block[:, :, None] * values
    stacked = jnp.concatenate([weight_in, value_in], axis=-1).transpose(1, 0, 2)
    solved = jnp.einsum("hij,hjd->hid", unit_lower_inverse(lower_part), stacked, precision=precise)
    key_width = key_rows.shape[-1]
    weight_rows = solved[:, :, :key_width]
    pseudo_values = solved[:, :, key_width:]
    attend = jnp.einsum("ihd,jhd->hij", queries, key_rows, precision=precise) * decay_incl
    query_decayed = ((growth * start_open[:, None])[:, :, None] * queries).transpose(1, 0, 2)
    tail_decay = jnp.exp(cumulative[-1][None, :] - cumulative) * end_open[:, None]
    key_decayed = (tail_decay[:, :, None] * key_rows).transpose(1, 0, 2)
    block_decay = jnp.exp(cumulative[-1]) * carries
    return (weight_rows, pseudo_values, attend, query_decayed, key_decayed, block_decay)


def gated_norm(outputs, gate_rows, gain_row):
    mean_square = jnp.mean(outputs * outputs, axis=-1, keepdims=True)
    normed = outputs * lax.rsqrt(mean_square + 1e-06) * gain_row
    gate_values = gate_rows.astype(jnp.float32).reshape(outputs.shape)
    return (normed * jax.nn.silu(gate_values)).astype(jnp.bfloat16).reshape(outputs.shape[0], -1)


def local(q_raw, k_raw, v_raw, conv_weight, gate_log, beta, gate_z, norm_gain, doc_start):
    length = q_raw.shape[0]
    margin = conv_weight.shape[0] - 1
    q_width = q_raw.shape[1]
    value_heads = gate_log.shape[1]
    rim_query, rim_key, rim_value = passed_along(
        (q_raw[length - margin :], k_raw[length - margin :], v_raw[length - margin :]), "ctx", 1
    )
    places = jnp.arange(length, dtype=jnp.int32)
    slab_docs = (places >= doc_start[0]).astype(jnp.int32)
    rim_docs = jnp.zeros((margin,), jnp.int32)
    query_conv = conv_silu(q_raw, rim_query, slab_docs, rim_docs, conv_weight[:, :q_width])
    key_conv = conv_silu(k_raw, rim_key, slab_docs, rim_docs, conv_weight[:, q_width : 2 * q_width])
    value_conv = conv_silu(v_raw, rim_value, slab_docs, rim_docs, conv_weight[:, 2 * q_width :])
    blocks = length // SPAN
    eye_keys = jnp.eye(DK, dtype=jnp.float32)

    def advance(chain_carry, inputs):
        prior_doc, through, offset_state = chain_carry
        query_block, key_block, value_block, gate_block, beta_block, block_docs = inputs
        terms = block_terms(
            query_block, key_block, value_block, gate_block, beta_block, block_docs, prior_doc
        )
        weight_rows, pseudo_values, attend, query_decayed, key_decayed, block_decay = terms
        query_state = query_decayed - jnp.einsum(
            "hij,hjk->hik", attend, weight_rows, precision=precise
        )
        local_out = jnp.einsum("hij,hjv->ihv", attend, pseudo_values, precision=precise)
        local_out = local_out + jnp.einsum(
            "hck,hvk->chv", query_state, offset_state, precision=precise
        )
        reaching = jnp.einsum("hck,hkj->chj", query_state, through, precision=precise)
        transition = block_decay[:, None, None] * eye_keys[None] - jnp.einsum(
            "hck,hcj->hkj", key_decayed, weight_rows, precision=precise
        )
        written = jnp.einsum("hcv,hck->hvk", pseudo_values, key_decayed, precision=precise)
        through = jnp.einsum("hkj,hjl->hkl", transition, through, precision=precise)
        offset_state = (
            jnp.einsum("hvk,hjk->hvj", offset_state, transition, precision=precise) + written
        )
        return ((block_docs[-1], through, offset_state), (local_out, reaching))

    initial = (
        jnp.zeros((), jnp.int32),
        jnp.broadcast_to(eye_keys, (value_heads, DK, DK)),
        jnp.zeros((value_heads, DV, DK), jnp.float32),
    )
    inputs = (
        query_conv.reshape(blocks, SPAN, -1),
        key_conv.reshape(blocks, SPAN, -1),
        value_conv.reshape(blocks, SPAN, -1),
        gate_log.reshape(blocks, SPAN, value_heads),
        beta.reshape(blocks, SPAN, value_heads),
        slab_docs.reshape(blocks, SPAN),
    )
    (_, slab_map, slab_offset), (local_out, reaching) = lax.scan(advance, initial, inputs)
    device_count = lax.axis_size("ctx")
    per_head = device_count // value_heads
    row_count = DV // per_head
    maps_out = jnp.repeat(slab_map, per_head, axis=0)
    rows_out = slab_offset.reshape(device_count, row_count, DK)
    maps_in, rows_in = (
        lax.all_to_all(maps_out, "ctx", split_axis=0, concat_axis=0, tiled=True),
        lax.all_to_all(rows_out, "ctx", split_axis=0, concat_axis=0, tiled=True),
    )

    def pass_slab(memory, pair):
        one_map, one_rows = pair
        return (jnp.einsum("vk,jk->vj", memory, one_map, precision=precise) + one_rows, memory)

    _, entering = lax.scan(pass_slab, jnp.zeros((row_count, DK), jnp.float32), (maps_in, rows_in))
    returned = lax.all_to_all(entering, "ctx", split_axis=0, concat_axis=0, tiled=True)
    incoming = returned.reshape(value_heads, DV, DK)
    outputs = local_out + jnp.einsum("nchk,hvk->nchv", reaching, incoming, precision=precise)
    return gated_norm(outputs.reshape(length, value_heads, DV), gate_z, norm_gain)


def solution(mesh):
    return jax.shard_map(
        local,
        mesh=mesh,
        in_specs=(
            P(("groups", "ctx"), None),
            P(("groups", "ctx"), None),
            P(("groups", "ctx"), None),
            P(),
            P(("groups", "ctx"), None),
            P(("groups", "ctx"), None),
            P(("groups", "ctx"), None),
            P(),
            P(("groups", "ctx")),
        ),
        out_specs=P(("groups", "ctx"), None),
        check_vma=False,
    )
```

profile of v0, /device:TPU:29, one launch (start us, length us, event | category | flops | bytes accessed | tf_op | source)
XLA Modules:
  0.0 426.8 jit_solution(4907095991047330980)
XLA Ops:
  12.0 4.9 %multiply_convert_fusion.1 = bf16[512,1024]{1,0:T(8,128)(2,1)S(1)} fusion(bf16[512,1024]{1,0:T(8,128)(2,1)} %param.13, bf16[3,1024]{1,0:T(4,128)(2,1)S(1)} %collective-permute-done.2, f32[1024]{0:T(1024)S(1)} %bitcast.304, f32[1024]{0:T(1024)S(1)} %bitcast.305, f32[1024]{0:T(1024)S(1)} %bitcast.303, f32[1024]{0:T(1024)S(1)} %bitcast.302, ...), kind=kLoop, calls=%fused_computation.108 | loop fusion | flops 14680064 | bytes 2121216 | tf_op jit(solution)/shard_map/convert_element_type | solution.py:31
  17.0 2.8 multiply_convert_fusion.2
  19.8 5.0 %multiply_convert_fusion = bf16[512,2048]{1,0:T(8,128)(2,1)} fusion(bf16[512,2048]{1,0:T(8,128)(2,1)S(1)} %copy-done.8, bf16[3,2048]{1,0:T(4,128)(2,1)S(1)} %collective-permute-done.1, f32[2048]{0:T(1024)S(1)} %bitcast.295, f32[2048]{0:T(1024)S(1)} %bitcast.296, f32[2048]{0:T(1024)S(1)} %bitcast.297, f32[2048]{0:T(1024)S(1)} %bitcast.294, ...), kind=kLoop, calls=%fused_computation.101 | loop fusion | flops 29360128 | bytes 4240896 | tf_op jit(solution)/shard_map/convert_element_type | solution.py:31
  26.0 271.2 %while.32 = (s32[]{:T(128)}, s32[]{:T(128)}, f32[16,128,128]{2,1,0:T(8,128)}, f32[16,128,128]{1,2,0:T(8,128)}, f32[8,64,16,128]{3,1,0,2:T(8,128)}, /*index=5*/f3...) while((s32[]{:T(128)}, s32[]{:T(128)}, ...), condition=%wide.region_4.5_spmd.clone, body=%wide.region_0.4_spmd.clone.sunk | while | flops 2722103552 | bytes 65937656 | solution.py:147
  44.1 2.9 fusion.218
  50.8 2.8 convolution_add_fusion.5
  76.6 3.3 fusion.218
  82.5 2.4 convolution_bitcast_fusion.7
  84.9 2.8 convolution_add_fusion.5
  110.7 3.3 fusion.218
  118.9 2.8 convolution_add_fusion.5
  144.8 3.3 fusion.218
  150.6 2.4 convolution_bitcast_fusion.7
  153.0 2.8 convolution_add_fusion.5
  178.9 3.2 fusion.218
  187.1 2.8 convolution_add_fusion.5
  212.9 3.2 fusion.218
  221.2 2.8 convolution_add_fusion.5
  247.0 3.3 fusion.218
  255.3 2.8 convolution_add_fusion.5
  281.1 3.2 fusion.218
  289.3 2.8 convolution_add_fusion.5
  297.2 34.0 %all_to_all.15 = f32[16,128,128]{2,1,0:T(8,128)S(1)} all-to-all(f32[16,128,128]{2,1,0:T(8,128)} %get-tuple-element.103), channel_id=1, replica_groups=mesh['groups'=2,'ctx'=16] {'ctx'}, dimensions={0} | all-to-all | bytes 2097152 | tf_op jit(solution)/shard_map/all_to_all | solution.py:154
  331.2 5.9 %all-to-all-start.1 = ((f32[16,128,128]{1,2,0:T(8,128)}), f32[16,128,128]{1,2,0:T(8,128)S(1)}, u32[]{:S(2)}, u32[]{:S(2)}) async-start(f32[16,128,128]{1,2,0:T(8,128)} %get-tuple-element.104), calls=%async_computation.1 | async-start | bytes 2097152 | tf_op jit(solution)/shard_map/all_to_all | solution.py:155
  337.1 23.9 %all-to-all-done.1 = f32[16,128,128]{1,2,0:T(8,128)S(1)} async-done(((f32[16,128,128]{1,2,0:T(8,128)}), f32[16,128,128]{1,2,0:T(8,128)S(1)}, u32[]{:S(2)}, u32[]{:S(2)}) %all-to-all-start.1) | async-done | bytes 1048608 | tf_op jit(solution)/shard_map/all_to_all | solution.py:155
  361.0 15.5 %while.33 = (s32[]{:T(128)}, f32[128,128]{0,1:T(8,128)S(1)}, f32[16,128,128]{2,1,0:T(8,128)}, f32[16,128,128]{2,1,0:T(8,128)S(1)}, f32[16,128,128]{1,2,0:T(8,128)S(1)}, /*index=5*/s32[]{:T(128)}, s32[]{:T(128)}) while((s32[]{:T(128)}, f32[128,128]{0,1:T(8,128)S(1)}, f32[16,128,128]{2,1,0:T(8,128)}, f32[16,128,128]{2,1,0:T(8,128)S(1)}, ...), condition=%wide.region_6.7_spmd.clone, body=%wide.region_5.6_spmd.clone.sunk | while | flops 25214980 | bytes 788056 | solution.py:162
  376.5 5.9 %all-to-all-start.2 = ((f32[16,128,128]{2,1,0:T(8,128)}), f32[16,128,128]{2,1,0:T(8,128)S(1)}, u32[]{:S(2)}, u32[]{:S(2)}) async-start(f32[16,128,128]{2,1,0:T(8,128)} %get-tuple-element.105), calls=%async_computation.2 | async-start | bytes 2097152 | tf_op jit(solution)/shard_map/all_to_all | solution.py:163
  382.4 23.9 %all-to-all-done.2 = f32[16,128,128]{2,1,0:T(8,128)S(1)} async-done(((f32[16,128,128]{2,1,0:T(8,128)}), f32[16,128,128]{2,1,0:T(8,128)S(1)}, u32[]{:S(2)}, u32[]{:S(2)}) %all-to-all-start.2) | async-done | bytes 1048608 | tf_op jit(solution)/shard_map/all_to_all | solution.py:163
  406.3 5.5 %fusion.72 = f32[16,128,512]{1,2,0:S(1)} fusion(f32[16,128,128]{2,1,0:T(8,128)S(1)} %all-to-all-done.2, f32[16,128,512]{1,2,0:T(8,128)} %bitcast.287), kind=kOutput, calls=%fused_computation.142 | convolution fusion | flops 1610612736 | bytes 9437184
  411.8 3.0 multiply_reduce_fusion.2
  415.0 4.6 %copy.64 = f32[8,64,16,128]{3,2,1,0:T(8,128)S(1)} copy(f32[8,64,16,128]{3,1,0,2:T(8,128)} %get-tuple-element.205) | data formatting | bytes 8388608 | tf_op jit(solution)/shard_map/add | solution.py:165
  421.1 5.7 %fusion.54 = bf16[512,2048]{1,0:T(8,128)(2,1)} fusion(bf16[512,2048]{1,0:T(8,128)(2,1)S(1)} %copy-done.9, f32[64,8,16,128]{3,2,1,0:T(8,128)S(1)} %bitcast.284, f32[64,8,16,128]{3,2,1,0:T(8,128)S(1)} %bitcast.283, f32[2048]{0:T(1024)S(1)} %broadcast_bitcast_fusion), kind=kLoop, calls=%fused_computation.102 | loop fusion | flops 9437184 | bytes 12591104 | tf_op jit(solution)/shard_map/convert_element_type | solution.py:89
  (687 shorter events, 233.9 us)
Async XLA Ops:
  0.0 382.4 %copy-start = (f32[128]{0:T(128)S(1)}, f32[128]{0:T(128)}, u32[]{:S(2)}) copy-start(f32[128]{0:T(128)} %param.20) | copy-start | bytes 1540
  0.0 17.0 %copy-start.12 = (bf16[512,1024]{1,0:T(8,128)(2,1)S(1)}, bf16[512,1024]{1,0:T(8,128)(2,1)}, u32[]{:S(2)}) copy-start(bf16[512,1024]{1,0:T(8,128)(2,1)} %param.14) | copy-start | bytes 3145732
  0.8 11.2 %collective-permute-start.2 = (bf16[3,1024]{1,0:T(4,128)(2,1)S(1)}, bf16[3,1024]{1,0:T(4,128)(2,1)S(1)}, u32[]{:S(2)}, u32[]{:S(2)}) collective-permute-start(bf16[3,1024]{1,0:T(4,128)(2,1)S(1)} %slice.138), channel_id=1, source_target_pairs={{0,1},{1,2},{2,3},{3,4},{4,5},{5,6},{6,7},{7,8},{8,9},{9,10},{10,1... | collective-permute-start | bytes 18440 | tf_op jit(solution)/shard_map/ppermute | solution.py:19
  2.8 14.1 %collective-permute-start = (bf16[3,1024]{1,0:T(4,128)(2,1)S(1)}, bf16[3,1024]{1,0:T(4,128)(2,1)S(1)}, u32[]{:S(2)}, u32[]{:S(2)}) collective-permute-start(bf16[3,1024]{1,0:T(4,128)(2,1)S(1)} %slice.120), channel_id=1, source_target_pairs={{0,1},{1,2},{2,3},{3,4},{4,5},{5,6},{6,7},{7,8},{8,9},{9,10},{10,1... | collective-permute-start | bytes 18440 | tf_op jit(solution)/shard_map/ppermute | solution.py:19
  5.5 14.3 %collective-permute-start.1 = (bf16[3,2048]{1,0:T(4,128)(2,1)}, bf16[3,2048]{1,0:T(4,128)(2,1)S(1)}, u32[]{:S(2)}, u32[]{:S(2)}) collective-permute-start(bf16[3,2048]{1,0:T(4,128)(2,1)} %slice.130), channel_id=1, source_target_pairs={{0,1},{1,2},{2,3},{3,4},{4,5},{5,6},{6,7},{7,8},{8,9},{9,10},{10,1... | collective-permute-start | bytes 36872 | tf_op jit(solution)/shard_map/ppermute | solution.py:19
  9.5 7.5 %copy-start.13 = (pred[512]{0:T(512)(128)(4,1)}, pred[512]{0:T(512)(128)(4,1)S(1)}, u32[]{:S(2)}) copy-start(pred[512]{0:T(512)(128)(4,1)S(1)} %get-tuple-element.228) | copy-start | bytes 1540
  9.5 7.5 %copy-start.15 = (pred[512]{0:T(512)(128)(4,1)}, pred[512]{0:T(512)(128)(4,1)S(1)}, u32[]{:S(2)}) copy-start(pred[512]{0:T(512)(128)(4,1)S(1)} %get-tuple-element.229) | copy-start | bytes 1540
  9.5 7.5 %copy-start.17 = (pred[512]{0:T(512)(128)(4,1)}, pred[512]{0:T(512)(128)(4,1)S(1)}, u32[]{:S(2)}) copy-start(pred[512]{0:T(512)(128)(4,1)S(1)} %get-tuple-element.230) | copy-start | bytes 1540
  12.0 7.8 %copy-start.8 = (bf16[512,2048]{1,0:T(8,128)(2,1)S(1)}, bf16[512,2048]{1,0:T(8,128)(2,1)}, u32[]{:S(2)}) copy-start(bf16[512,2048]{1,0:T(8,128)(2,1)} %param.15) | copy-start | bytes 6291460
  26.0 3.4 copy-start.6
  26.0 11.4 %copy-start.10 = (f32[8,64,16]{2,1,0:T(8,128)}, f32[8,64,16]{2,1,0:T(8,128)S(1)}, u32[]{:S(2)}) copy-start(f32[8,64,16]{2,1,0:T(8,128)S(1)} %get-tuple-element.402) | copy-start | bytes 98308 | tf_op jit(solution)/shard_map/while
  50.8 2.8 copy-start.1
  58.5 3.5 copy-start.6
  58.5 11.4 %copy-start.10 = (f32[8,64,16]{2,1,0:T(8,128)}, f32[8,64,16]{2,1,0:T(8,128)S(1)}, u32[]{:S(2)}) copy-start(f32[8,64,16]{2,1,0:T(8,128)S(1)} %get-tuple-element.402) | copy-start | bytes 98308 | tf_op jit(solution)/shard_map/while
  92.6 3.5 copy-start.6
  92.6 11.4 %copy-start.10 = (f32[8,64,16]{2,1,0:T(8,128)}, f32[8,64,16]{2,1,0:T(8,128)S(1)}, u32[]{:S(2)}) copy-start(f32[8,64,16]{2,1,0:T(8,128)S(1)} %get-tuple-element.402) | copy-start | bytes 98308 | tf_op jit(solution)/shard_map/while
  126.7 3.5 copy-start.6
  126.7 11.4 %copy-start.10 = (f32[8,64,16]{2,1,0:T(8,128)}, f32[8,64,16]{2,1,0:T(8,128)S(1)}, u32[]{:S(2)}) copy-start(f32[8,64,16]{2,1,0:T(8,128)S(1)} %get-tuple-element.402) | copy-start | bytes 98308 | tf_op jit(solution)/shard_map/while
  153.0 2.8 copy-start.1
  160.7 3.5 copy-start.6
  160.7 11.4 %copy-start.10 = (f32[8,64,16]{2,1,0:T(8,128)}, f32[8,64,16]{2,1,0:T(8,128)S(1)}, u32[]{:S(2)}) copy-start(f32[8,64,16]{2,1,0:T(8,128)S(1)} %get-tuple-element.402) | copy-start | bytes 98308 | tf_op jit(solution)/shard_map/while
  187.1 2.8 copy-start.1
  194.8 3.5 copy-start.6
  194.8 11.4 %copy-start.10 = (f32[8,64,16]{2,1,0:T(8,128)}, f32[8,64,16]{2,1,0:T(8,128)S(1)}, u32[]{:S(2)}) copy-start(f32[8,64,16]{2,1,0:T(8,128)S(1)} %get-tuple-element.402) | copy-start | bytes 98308 | tf_op jit(solution)/shard_map/while
  221.2 2.8 copy-start.1
  228.9 3.5 copy-start.6
  228.9 11.4 %copy-start.10 = (f32[8,64,16]{2,1,0:T(8,128)}, f32[8,64,16]{2,1,0:T(8,128)S(1)}, u32[]{:S(2)}) copy-start(f32[8,64,16]{2,1,0:T(8,128)S(1)} %get-tuple-element.402) | copy-start | bytes 98308 | tf_op jit(solution)/shard_map/while
  263.0 3.5 copy-start.6
  263.0 11.4 %copy-start.10 = (f32[8,64,16]{2,1,0:T(8,128)}, f32[8,64,16]{2,1,0:T(8,128)S(1)}, u32[]{:S(2)}) copy-start(f32[8,64,16]{2,1,0:T(8,128)S(1)} %get-tuple-element.402) | copy-start | bytes 98308 | tf_op jit(solution)/shard_map/while
  331.2 29.8 %all-to-all-start.1 = ((f32[16,128,128]{1,2,0:T(8,128)}), f32[16,128,128]{1,2,0:T(8,128)S(1)}, u32[]{:S(2)}, u32[]{:S(2)}) async-start(f32[16,128,128]{1,2,0:T(8,128)} %get-tuple-element.104), calls=%async_computation.1 | async-start | bytes 2097152 | tf_op jit(solution)/shard_map/all_to_all | solution.py:155
  376.5 29.8 %all-to-all-start.2 = ((f32[16,128,128]{2,1,0:T(8,128)}), f32[16,128,128]{2,1,0:T(8,128)S(1)}, u32[]{:S(2)}, u32[]{:S(2)}) async-start(f32[16,128,128]{2,1,0:T(8,128)} %get-tuple-element.105), calls=%async_computation.2 | async-start | bytes 2097152 | tf_op jit(solution)/shard_map/all_to_all | solution.py:163
  406.3 5.5 %copy-start.3 = (f32[8,64,16,128]{3,1,0,2:T(8,128)S(1)}, f32[8,64,16,128]{3,1,0,2:T(8,128)}, u32[]{:S(2)}) copy-start(f32[8,64,16,128]{3,1,0,2:T(8,128)} %get-tuple-element.102) | copy-start | bytes 12582916
  (48 other events, 92.8 us)
where the time goes:
time: 431 us; the launch traced here: 427 us
  matrix products  217 us (50%)
  other arithmetic  53.1 us (12%)
  waiting for transfers between devices  47.9 us (11%)
  local copies, waits for them, and re-layouts  44.6 us (10%)
  blocking collectives  34 us (8%)
  starting transfers between devices  15.6 us (4%)
  loops' own time  13.7 us (3%)
    all_to_all x1, blocking collectives, local(): lax.all_to_all(maps_out, 'ctx', split_axis=0, concat_axis=0, tiled=True)  34 us
    dot_general x40, matrix products, unit_lower_inverse(): power = jnp.einsum('hij,hjk->hik', power, power, precision=precise)  26.3 us
    dot_general x40, matrix products, unit_lower_inverse(): jnp.einsum('hij,hjk->hik', inverse, eye_rows + power, precision=precise)  26.2 us
    dot_general x8, matrix products, advance(): jnp.einsum('hck,hvk->chv', query_state, offset_state, precision=precise)  25.7 us
    all_to_all x1, waiting for transfers between devices, local(): lax.all_to_all(rows_out, 'ctx', split_axis=0, concat_axis=0, tiled=True)  23.9 us
    all_to_all x1, waiting for transfers between devices, local(): lax.all_to_all(entering, 'ctx', split_axis=0, concat_axis=0, tiled=True)  23.9 us
    dot_general x8, matrix products, advance(): jnp.einsum('hcv,hck->hvk', pseudo_values, key_decayed, precision=precise)  22.7 us
    dot_general x8, matrix products, advance(): jnp.einsum('hvk,hjk->hvj', offset_state, transition, precision=precise)  17.9 us
  transfers between devices with their start and end apart: 5, of which 2 were waited for; matrix products, arithmetic and copies ran while one was open for 3% of the time, Pallas kernels for 0%

commit v1 on v0

v1 whole, which is shorter than its diff:
```python
import functools

import jax
import jax.numpy as jnp
from jax import lax
from jax.experimental import pallas as pl
from jax.experimental.pallas import tpu as pltpu
from jax.sharding import PartitionSpec as P

HK = 8
HV = 16
DK = 128
DV = 128
CH = 128
RIM = 16
f32 = jnp.float32
bf16 = jnp.bfloat16


def split(x):
    hi = x.astype(bf16)
    return hi, (x - hi.astype(f32)).astype(bf16)


def mm(a, b):
    return lax.dot_general(a, b, (((1,), (0,)), ((), ())), preferred_element_type=f32)


def mm_nt(a, b):
    return lax.dot_general(a, b, (((1,), (1,)), ((), ())), preferred_element_type=f32)


def nt3(a, b):
    ah, al = split(a)
    bh, bl = split(b)
    return mm_nt(ah, bh) + mm_nt(al, bh) + mm_nt(ah, bl)


def mm3(ah, al, bh, bl):
    left = jnp.concatenate([ah, al], axis=1)
    return mm(left, jnp.concatenate([bh, bh], axis=0)) + mm(ah, bl)


def conv(ext, raw, rim, w, since, length):
    width = raw.shape[1]
    ext[0:RIM, 0:width] = rim.astype(f32)
    ext[RIM : RIM + length, 0:width] = raw.astype(f32)
    taps = w.shape[0]
    total = None
    for s in range(taps):
        back = taps - 1 - s
        term = ext[RIM - back : RIM - back + length, 0:width] * w[s : s + 1, :]
        if back:
            term = jnp.where(since < back, 0.0, term)
        total = term if total is None else total + term
    return (total / (1.0 + jnp.exp(-total))).astype(bf16)


def slab_kernel(
    doc, q, k, v, rq, rk, rv, wq, wk, wv, cumc, cumr, betac, betar, loc, reach, smap, soff, ext
):
    length = q.shape[0]
    sd = doc[0]
    row = lax.broadcasted_iota(jnp.int32, (length, DK), 0) - sd
    since = jnp.where(row < 0, length + 8, row)
    qc = conv(ext, q[...], rq[...], wq[...], since, length)
    kc = conv(ext, k[...], rk[...], wk[...], since, length)
    since2 = jnp.concatenate([since, since], axis=1)
    vc = conv(ext, v[...], rv[...], wv[...], since2, length)
    chunks = length // CH
    ii = lax.broadcasted_iota(jnp.int32, (CH, CH), 0)
    jj = lax.broadcasted_iota(jnp.int32, (CH, CH), 1)
    ix = ii ^ jj
    eye = ii == jj
    eyef = jnp.where(eye, 1.0, 0.0)
    tcol = lax.broadcasted_iota(jnp.int32, (CH, 1), 0)
    shared = []
    lowers = []
    per = []
    for c in range(chunks):
        b = c * CH
        kcc, qcc = kc[b : b + CH], qc[b : b + CH]
        kq = jnp.concatenate([kcc, qcc], axis=0)
        gram = mm_nt(kq, kcc)
        kk = jnp.where(eye, gram[:CH], 0.0)
        k_row = lax.rsqrt(jnp.sum(kk, axis=0, keepdims=True) + 1e-6)
        k_col = lax.rsqrt(jnp.sum(kk, axis=1, keepdims=True) + 1e-6)
        qf = qcc.astype(f32)
        q_col = lax.rsqrt(jnp.sum(qf * qf, axis=1, keepdims=True) + 1e-6) * (DK**-0.5)
        same = (ii + b >= sd) == (jj + b >= sd)
        mask = jnp.where((ii >= jj) & same, 0.0, -1e30)
        gs = gram[:CH] * k_col * k_row
        ats = gram[CH:] * q_col * k_row
        opened = jnp.where((tcol + b >= sd) & (b - 1 < sd), 0.0, 1.0)
        ended = jnp.where((tcol + b < sd) & (b + CH - 1 >= sd), 0.0, 1.0)
        carries = jnp.where((b + CH - 1 >= sd) & (b - 1 < sd), 0.0, 1.0)
        kt = kcc.astype(f32).T.astype(bf16)
        shared.append((jnp.concatenate([kq, kq], axis=1), jnp.concatenate([kt, kt], axis=1)))
        for e in range(2):
            cc = cumc[0, b : b + CH, e : e + 1]
            cr = cumr[0, e : e + 1, b : b + CH]
            bc = betac[0, b : b + CH, e : e + 1]
            br = betar[0, e : e + 1, b : b + CH]
            decay = jnp.exp(cc - cr + mask)
            lower = gs * decay * bc
            att = ats * decay
            growth = jnp.exp(cc) * opened
            last = cc[CH - 1 : CH]
            tail = jnp.exp(last - cc) * ended * k_col
            lowers.append(lower)
            per.append(
                (
                    jnp.concatenate(split(att), axis=1),
                    growth * k_col,
                    growth * q_col,
                    tail,
                    jnp.exp(last) * carries,
                    br,
                )
            )
    count = len(lowers)
    inv = [eyef - jnp.where(ix == 1, lw, 0.0) for lw in lowers]
    lsp = [split(lw) for lw in lowers]
    for lm in range(1, (CH - 1).bit_length()):
        pick = (ix >> lm) == 1
        zero = jnp.zeros((CH, CH), bf16)
        tsp = [split(t) for t in inv]
        low = [(jnp.where(pick, a, zero), jnp.where(pick, d, zero)) for a, d in lsp]
        es = [mm3(*low[n], *tsp[n]) for n in range(count)]
        esp = [split(x) for x in es]
        inv = [inv[n] - mm3(*tsp[n], *esp[n]) for n in range(count)]
    states = [jnp.concatenate([eyef, jnp.zeros((DK, DV), f32)], axis=1) for _ in range(2)]
    for c in range(chunks):
        b = c * CH
        kqkq, ktkt = shared[c]
        for e in range(2):
            att, gk, gq, tail, dec, br = per[2 * c + e]
            x = states[e]
            u = mm(kqkq, jnp.concatenate(split(x), axis=0))
            uk = u[:CH] * gk
            vcc = vc[b : b + CH, e * DV : (e + 1) * DV].astype(f32)
            r = jnp.concatenate([-uk[:, :DK], vcc - uk[:, DK:]], axis=1)
            fresh = mm3(*split(inv[2 * c + e] * br), *split(r))
            fh = fresh.astype(bf16)
            o = u[CH:] * gq + mm(att, jnp.concatenate([fh, fh], axis=0))
            reach[b : b + CH, e * DK : (e + 1) * DK] = o[:, :DK]
            loc[b : b + CH, e * DV : (e + 1) * DV] = o[:, DK:]
            states[e] = x * dec + mm(ktkt, jnp.concatenate(split(fresh * tail), axis=0))
    for e in range(2):
        smap[e] = states[e][:, :DK]
        soff[e] = states[e][:, DK:].T


def pass_kernel(maps, rows, entering):
    count = maps.shape[0]

    def step(d, s):
        entering[d] = s
        return nt3(s, maps[d]) + rows[d]

    lax.fori_loop(0, count, step, jnp.zeros(rows.shape[1:], f32))


def out_kernel(loc, reach, state, z, gain, out):
    for e in range(2):
        cols = slice(e * DV, (e + 1) * DV)
        o = loc[:, cols] + nt3(reach[:, cols], state[e])
        ms = jnp.mean(o * o, axis=-1, keepdims=True)
        zf = z[:, cols].astype(f32)
        gated = o * lax.rsqrt(ms + 1e-6) * gain[...] * (zf / (1.0 + jnp.exp(-zf)))
        out[:, cols] = gated.astype(bf16)


def local(q_raw, k_raw, v_raw, conv_weight, gate_log, beta, gate_z, norm_gain, doc_start):
    length = q_raw.shape[0]
    taps = conv_weight.shape[0]
    n = lax.axis_size("ctx")
    pairs = [(i, i + 1) for i in range(n - 1)]
    rims = lax.ppermute(
        (q_raw[length - RIM :], k_raw[length - RIM :], v_raw[length - RIM :]), "ctx", pairs
    )
    chunks = length // CH
    cum = jnp.cumsum(gate_log.reshape(chunks, CH, HV), axis=1).reshape(length, HK, 2)
    bet = beta.reshape(length, HK, 2)
    cumc, cumr = cum.transpose(1, 0, 2), cum.transpose(1, 2, 0)
    betac, betar = bet.transpose(1, 0, 2), bet.transpose(1, 2, 0)
    params = pltpu.CompilerParams(vmem_limit_bytes=50 * 1024 * 1024)
    col1 = lambda rows, off=0: pl.BlockSpec((rows, DK), lambda g, off=off: (0, g + off))
    col2 = lambda rows, off=0: pl.BlockSpec((rows, 2 * DV), lambda g, off=off: (0, g + off))
    cspec = pl.BlockSpec((1, length, 2), lambda g: (g, 0, 0))
    rspec = pl.BlockSpec((1, 2, length), lambda g: (g, 0, 0))
    mspec = pl.BlockSpec((2, DK, DK), lambda g: (g, 0, 0))
    loc, reach, smap, soff = pl.pallas_call(
        slab_kernel,
        grid=(HK,),
        in_specs=[
            pl.BlockSpec(memory_space=pltpu.SMEM),
            col1(length), col1(length), col2(length),
            col1(RIM), col1(RIM), col2(RIM),
            col1(taps), col1(taps, HK), col2(taps, HK),
            cspec, rspec, cspec, rspec,
        ],
        out_specs=[col2(length), col2(length), mspec, mspec],
        out_shape=[
            jax.ShapeDtypeStruct((length, HV * DV), f32),
            jax.ShapeDtypeStruct((length, HV * DK), f32),
            jax.ShapeDtypeStruct((HV, DK, DK), f32),
            jax.ShapeDtypeStruct((HV, DV, DK), f32),
        ],
        scratch_shapes=[pltpu.VMEM((length + RIM, 2 * DV), f32)],
        compiler_params=params,
    )(
        doc_start, q_raw, k_raw, v_raw, *rims, conv_weight, conv_weight, conv_weight,
        cumc, cumr, betac, betar,
    )
    per_head = n // HV
    rc = DV // per_head
    maps_out = jnp.repeat(smap, per_head, axis=0)
    rows_out = soff.reshape(n, rc, DK)
    maps_in = lax.all_to_all(maps_out, "ctx", split_axis=0, concat_axis=0, tiled=True)
    rows_in = lax.all_to_all(rows_out, "ctx", split_axis=0, concat_axis=0, tiled=True)
    entering = pl.pallas_call(
        pass_kernel,
        out_shape=jax.ShapeDtypeStruct((n, rc, DK), f32),
        compiler_params=params,
    )(maps_in, rows_in)
    back = lax.all_to_all(entering, "ctx", split_axis=0, concat_axis=0, tiled=True)
    state = back.reshape(HV, DV, DK)
    return pl.pallas_call(
        out_kernel,
        grid=(HK,),
        in_specs=[
            col2(length), col2(length), mspec, col2(length),
            pl.BlockSpec((1, DV), lambda g: (0, 0)),
        ],
        out_specs=col2(length),
        out_shape=jax.ShapeDtypeStruct((length, HV * DV), bf16),
        compiler_params=params,
    )(loc, reach, state, gate_z, norm_gain.reshape(1, DV))


def solution(mesh):
    rows = P(("groups", "ctx"), None)
    return jax.shard_map(
        local,
        mesh=mesh,
        in_specs=(rows, rows, rows, P(), rows, rows, rows, P(), P(("groups", "ctx"))),
        out_specs=rows,
        check_vma=False,
    )
```

time: 431 us -> 178 us (0.41)
  matrix products: 217 us -> 0 us
  Pallas kernels: 0 us -> 68.9 us
  blocking collectives: 34 us -> 93.1 us
  other arithmetic: 53.1 us -> 0.26 us
  waiting for transfers between devices: 47.9 us -> 0.01 us
  local copies, waits for them, and re-layouts: 44.6 us -> 8.2 us
  loops' own time: 13.7 us -> 0 us
  starting transfers between devices: 15.6 us -> 3.84 us
    dot_general x184 -> x0, matrix products: 212 us -> none  [the longest x40 26.3 us: unit_lower_inverse(): power = jnp.einsum('hij,hjk->hik', power, power, precision=precise)]
    pallas_call x0 -> x3, Pallas kernels: none -> 68.9 us  [the longest x1 56.5 us: local(): pl.pallas_call(slab_kernel, grid=(HK,), in_specs=[pl.BlockSpec(memory_spa...]
    all_to_all x0 -> x2, blocking collectives: none -> 59.3 us  [the longest x1 29.7 us: local(): lax.all_to_all(entering, 'ctx', split_axis=0, concat_axis=0, tiled=True)]
    all_to_all x2 -> x0, waiting for transfers between devices: 47.9 us -> none  [the longest x1 23.9 us: local(): lax.all_to_all(rows_out, 'ctx', split_axis=0, concat_axis=0, tiled=True)]
    convert_element_type x39 -> x0, other arithmetic: 23.7 us -> none  [the longest x3 12.7 us: conv_silu(): return jax.nn.silu(summed).astype(jnp.bfloat16)]
    while x16 -> x0, other arithmetic: 14.7 us -> none
    another operation x2 -> x0, loops' own time: 13.7 us -> none  [the longest x1 13.4 us: local(): lax.scan(advance, initial, inputs)]
    all_to_all x2 -> x0, starting transfers between devices: 11.7 us -> none  [the longest x1 5.87 us: local(): lax.all_to_all(entering, 'ctx', split_axis=0, concat_axis=0, tiled=True)]
  transfers between devices with their start and end apart: 5 -> 3, of which waited for: 2 -> 0; matrix products, arithmetic and copies ran while one was open for 3% -> 4% of each run, Pallas kernels for 0% -> 0%
where the time goes in v1:
time: 178 us; the launch traced here: 175 us
  blocking collectives  93.1 us (52%)
  Pallas kernels  68.9 us (39%)
  local copies, waits for them, and re-layouts  8.2 us (5%)
  starting transfers between devices  3.84 us (2%)
    pallas_call x1, Pallas kernels, local(): pl.pallas_call(slab_kernel, grid=(HK,), in_specs=[pl.BlockSpec(memory_spa...  56.5 us
    all_to_all x1, blocking collectives, local(): lax.all_to_all(maps_out, 'ctx', split_axis=0, concat_axis=0, tiled=True)  33.8 us
    all_to_all x1, blocking collectives, local(): lax.all_to_all(entering, 'ctx', split_axis=0, concat_axis=0, tiled=True)  29.7 us
    all_to_all x1, blocking collectives, local(): lax.all_to_all(rows_out, 'ctx', split_axis=0, concat_axis=0, tiled=True)  29.6 us
    pallas_call x1, Pallas kernels, local(): pl.pallas_call(out_kernel, grid=(HK,), in_specs=[col2(length), col2(lengt...  9.18 us
    ppermute x3, starting transfers between devices, local(): lax.ppermute((q_raw[length - RIM:], k_raw[length - RIM:], v_raw[length -...  3.84 us
  transfers between devices with their start and end apart: 3, of which 0 were waited for; matrix products, arithmetic and copies ran while one was open for 4% of the time, Pallas kernels for 0%

profile of v1, /device:TPU:29, one launch (start us, length us, event | category | flops | bytes accessed | tf_op | source)
XLA Modules:
  0.0 175.0 jit_solution(5357269026443130254)
XLA Ops:
  0.0 0.8 slice.11
  0.8 1.3 collective-permute-start.2
  2.1 0.8 slice.10
  2.9 1.3 collective-permute-start.1
  4.2 0.8 slice.9
  5.0 1.3 collective-permute-start
  6.9 0.8 reshape.14
  7.7 0.9 copy.14
  8.6 0.3 reduce_window_sum.11
  8.8 0.1 copy.11
  9.0 0.0 copy-start.1
  9.0 0.0 copy-start.2
  9.0 2.0 %copy.12.cumc = f32[8,512,2]{2,1,0:T(8,128)} copy(f32[8,512,2]{1,2,0:T(2,128)S(1)} %bitcast.12) | data formatting | bytes 65536 | tf_op jit(solution)/shard_map/transpose | solution.py:185
  11.0 2.0 %copy.13.betac = f32[8,512,2]{2,1,0:T(8,128)} copy(f32[8,512,2]{1,2,0:T(2,128)S(1)} %bitcast.10) | data formatting | bytes 65536 | tf_op jit(solution)/shard_map/transpose | solution.py:186
  13.0 0.0 collective-permute-done.1.rk
  13.0 0.0 collective-permute-done.rq
  13.0 0.0 collective-permute-done.2.rv
  13.0 0.0 copy-done.1
  13.0 0.0 copy-done.2
  13.0 56.5 %shard_map.91 = (f32[512,2048]{1,0:T(8,128)}, f32[512,2048]{1,0:T(8,128)}, f32[16,128,128]{2,1,0:T(8,128)S(1)}, f32[16,128,128]{2,1,0:T(8,128)S(1)}) custom-call(s32[1]{0:T(128)S(6)} %copy.15.doc, bf16[512,1024]{1,0:T(8,128)(2,1)S(1)} %copy-done.1, bf16[512,1024]{1,0:T(8,128)(2,1)} %k.1, bf16[512,2048]{1,0:T(8,128)(2,1)} %v.1, ...), custom_call_target="tpu_custom_call" | custom-call | tf_op jit(solution)/shard_map/pallas_call | solution.py:193
  69.6 33.8 %all_to_all.15.maps = f32[16,128,128]{2,1,0:T(8,128)S(1)} all-to-all(f32[16,128,128]{2,1,0:T(8,128)S(1)} %get-tuple-element.11), channel_id=1, replica_groups=mesh['groups'=2,'ctx'=16] {'ctx'}, dimensions={0} | all-to-all | bytes 2097152 | tf_op jit(solution)/shard_map/all_to_all | solution.py:220
  103.4 29.6 %all_to_all.16.rows = f32[16,128,128]{2,1,0:T(8,128)S(1)} all-to-all(f32[16,128,128]{2,1,0:T(8,128)S(1)} %get-tuple-element.12), channel_id=1, replica_groups=mesh['groups'=2,'ctx'=16] {'ctx'}, dimensions={0} | all-to-all | bytes 2097152 | tf_op jit(solution)/shard_map/all_to_all | solution.py:221
  133.0 0.0 copy-start
  133.0 0.0 copy-start.3
  133.0 3.2 %shard_map.92 = f32[16,128,128]{2,1,0:T(8,128)S(1)} custom-call(f32[16,128,128]{2,1,0:T(8,128)S(1)} %all_to_all.15.maps, f32[16,128,128]{2,1,0:T(8,128)S(1)} %all_to_all.16.rows), custom_call_target="tpu_custom_call" | custom-call | tf_op jit(solution)/shard_map/pallas_call | solution.py:222
  136.2 29.7 %all_to_all.17.state = f32[16,128,128]{2,1,0:T(8,128)S(1)} all-to-all(f32[16,128,128]{2,1,0:T(8,128)S(1)} %shard_map.92), channel_id=1, replica_groups=mesh['groups'=2,'ctx'=16] {'ctx'}, dimensions={0} | all-to-all | bytes 2097152 | tf_op jit(solution)/shard_map/all_to_all | solution.py:227
  165.9 0.0 copy-done
  165.9 0.0 copy-done.3
  165.9 9.2 %shard_map.93 = bf16[512,2048]{1,0:T(8,128)(2,1)} custom-call(f32[512,2048]{1,0:T(8,128)} %get-tuple-element.9.loc, f32[512,2048]{1,0:T(8,128)} %get-tuple-element.10.reach, f32[16,128,128]{2,1,0:T(8,128)S(1)} %all_to_all.17.state, bf16[512,2048]{1,0:T(8,128)(2,1)S(1)} %copy-done, f32[1,128]{1,0:T(1,128)S(1)} %bitcast.14), custom_call_target="tpu_custom_call" | custom-call | tf_op jit(solution)/shard_map/pallas_call | solution.py:229
  (1 shorter events, 0.0 us)
Async XLA Ops:
  0.8 12.2 %collective-permute-start.2 = (bf16[16,2048]{1,0:T(8,128)(2,1)S(1)}, bf16[16,2048]{1,0:T(8,128)(2,1)S(1)}, u32[]{:S(2)}, u32[]{:S(2)}) collective-permute-start(bf16[16,2048]{1,0:T(8,128)(2,1)S(1)} %slice.11), channel_id=1, source_target_pairs={{0,1},{1,2},{2,3},{3,4},{4,5},{5,6},{6,7},{7,8},{8,9},{9,10},{10,1... | collective-permute-start | bytes 196616 | tf_op jit(solution)/shard_map/ppermute | solution.py:179
  2.9 10.1 %collective-permute-start.1 = (bf16[16,1024]{1,0:T(8,128)(2,1)S(1)}, bf16[16,1024]{1,0:T(8,128)(2,1)S(1)}, u32[]{:S(2)}, u32[]{:S(2)}) collective-permute-start(bf16[16,1024]{1,0:T(8,128)(2,1)S(1)} %slice.10), channel_id=1, source_target_pairs={{0,1},{1,2},{2,3},{3,4},{4,5},{5,6},{6,7},{7,8},{8,9},{9,10},{10,1... | collective-permute-start | bytes 98312 | tf_op jit(solution)/shard_map/ppermute | solution.py:179
  5.0 8.1 %collective-permute-start = (bf16[16,1024]{1,0:T(8,128)(2,1)S(1)}, bf16[16,1024]{1,0:T(8,128)(2,1)S(1)}, u32[]{:S(2)}, u32[]{:S(2)}) collective-permute-start(bf16[16,1024]{1,0:T(8,128)(2,1)S(1)} %slice.9), channel_id=1, source_target_pairs={{0,1},{1,2},{2,3},{3,4},{4,5},{5,6},{6,7},{7,8},{8,9},{9,10},{10,1... | collective-permute-start | bytes 98312 | tf_op jit(solution)/shard_map/ppermute | solution.py:179
  9.0 4.0 %copy-start.1 = (bf16[512,1024]{1,0:T(8,128)(2,1)S(1)}, bf16[512,1024]{1,0:T(8,128)(2,1)}, u32[]{:S(2)}) copy-start(bf16[512,1024]{1,0:T(8,128)(2,1)} %q.1) | copy-start | bytes 3145732
  9.0 4.0 %copy-start.2 = (f32[4,4096]{1,0:T(4,128)S(1)}, f32[4,4096]{1,0:T(4,128)}, u32[]{:S(2)}) copy-start(f32[4,4096]{1,0:T(4,128)} %wv.1) | copy-start | bytes 196612
  133.0 32.9 %copy-start = (bf16[512,2048]{1,0:T(8,128)(2,1)S(1)}, bf16[512,2048]{1,0:T(8,128)(2,1)}, u32[]{:S(2)}) copy-start(bf16[512,2048]{1,0:T(8,128)(2,1)} %z.1) | copy-start | bytes 6291460
  133.0 32.9 %copy-start.3 = (f32[128]{0:T(128)S(1)}, f32[128]{0:T(128)}, u32[]{:S(2)}) copy-start(f32[128]{0:T(128)} %param.16) | copy-start | bytes 1540

commit v2 on v1

v2 whole, which is shorter than its diff:
```python
import functools

import jax
import jax.numpy as jnp
from jax import lax
from jax.experimental import pallas as pl
from jax.experimental.pallas import tpu as pltpu
from jax.sharding import PartitionSpec as P

HK = 8
HV = 16
DK = 128
DV = 128
CH = 128
RIM = 16
f32 = jnp.float32
bf16 = jnp.bfloat16


def split(x):
    hi = x.astype(bf16)
    return hi, (x - hi.astype(f32)).astype(bf16)


def mm(a, b):
    return lax.dot_general(a, b, (((1,), (0,)), ((), ())), preferred_element_type=f32)


def mm_nt(a, b):
    return lax.dot_general(a, b, (((1,), (1,)), ((), ())), preferred_element_type=f32)


def mm3(ah, al, bh, bl):
    left = jnp.concatenate([ah, al], axis=1)
    return mm(left, jnp.concatenate([bh, bh], axis=0)) + mm(ah, bl)


def conv(ext, raw, rim, w, since, length):
    width = raw.shape[1]
    ext[0:RIM, 0:width] = rim.astype(f32)
    ext[RIM : RIM + length, 0:width] = raw.astype(f32)
    taps = w.shape[0]
    total = None
    for s in range(taps):
        back = taps - 1 - s
        term = ext[RIM - back : RIM - back + length, 0:width] * w[s : s + 1, :]
        if back:
            term = jnp.where(since < back, 0.0, term)
        total = term if total is None else total + term
    return (total / (1.0 + jnp.exp(-total))).astype(bf16)


def slab(g, doc, q, k, v, rq, rk, rv, wq, wk, wv, cumc, cumr, betac, betar, loc, reach, ext):
    length = q.shape[0]
    one = pl.multiple_of(g * DK, DK)
    two = pl.multiple_of(g * 2 * DV, 2 * DV)
    sd = doc[0]
    row = lax.broadcasted_iota(jnp.int32, (length, DK), 0) - sd
    since = jnp.where(row < 0, length + 8, row)
    qc = conv(ext, q[...], rq[:, pl.ds(one, DK)], wq[...], since, length)
    kc = conv(ext, k[...], rk[:, pl.ds(one, DK)], wk[...], since, length)
    since2 = jnp.concatenate([since, since], axis=1)
    vc = conv(ext, v[...], rv[:, pl.ds(two, 2 * DV)], wv[...], since2, length)
    chunks = length // CH
    ii = lax.broadcasted_iota(jnp.int32, (CH, CH), 0)
    jj = lax.broadcasted_iota(jnp.int32, (CH, CH), 1)
    ix = ii ^ jj
    eye = ii == jj
    eyef = jnp.where(eye, 1.0, 0.0)
    tcol = lax.broadcasted_iota(jnp.int32, (CH, 1), 0)
    shared = []
    lowers = []
    per = []
    for c in range(chunks):
        b = c * CH
        kcc, qcc = kc[b : b + CH], qc[b : b + CH]
        kq = jnp.concatenate([kcc, qcc], axis=0)
        gram = mm_nt(kq, kcc)
        kk = jnp.where(eye, gram[:CH], 0.0)
        k_row = lax.rsqrt(jnp.sum(kk, axis=0, keepdims=True) + 1e-6)
        k_col = lax.rsqrt(jnp.sum(kk, axis=1, keepdims=True) + 1e-6)
        qf = qcc.astype(f32)
        q_col = lax.rsqrt(jnp.sum(qf * qf, axis=1, keepdims=True) + 1e-6) * (DK**-0.5)
        same = (ii + b >= sd) == (jj + b >= sd)
        mask = jnp.where((ii >= jj) & same, 0.0, -1e30)
        gs = gram[:CH] * k_col * k_row
        ats = gram[CH:] * q_col * k_row
        opened = jnp.where((tcol + b >= sd) & (b - 1 < sd), 0.0, 1.0)
        ended = jnp.where((tcol + b < sd) & (b + CH - 1 >= sd), 0.0, 1.0)
        carries = jnp.where((b + CH - 1 >= sd) & (b - 1 < sd), 0.0, 1.0)
        kt = kcc.astype(f32).T.astype(bf16)
        shared.append((jnp.concatenate([kq, kq], axis=1), jnp.concatenate([kt, kt], axis=1)))
        for e in range(2):
            cc = cumc[g, b : b + CH, e : e + 1]
            cr = cumr[g, e : e + 1, b : b + CH]
            bc = betac[g, b : b + CH, e : e + 1]
            br = betar[g, e : e + 1, b : b + CH]
            decay = jnp.exp(cc - cr + mask)
            lower = gs * decay * bc
            att = ats * decay
            growth = jnp.exp(cc) * opened
            last = cc[CH - 1 : CH]
            tail = jnp.exp(last - cc) * ended * k_col
            lowers.append(lower)
            per.append(
                (
                    jnp.concatenate([att.astype(bf16)] * 2, axis=1),
                    growth * k_col,
                    growth * q_col,
                    tail,
                    jnp.exp(last) * carries,
                    br,
                )
            )
    count = len(lowers)
    inv = [eyef - jnp.where(ix == 1, lw, 0.0) for lw in lowers]
    lsp = [split(lw) for lw in lowers]
    for lm in range(1, (CH - 1).bit_length()):
        pick = (ix >> lm) == 1
        zero = jnp.zeros((CH, CH), bf16)
        tsp = [split(t) for t in inv]
        low = [(jnp.where(pick, a, zero), jnp.where(pick, d, zero)) for a, d in lsp]
        es = [mm3(*low[n], *tsp[n]) for n in range(count)]
        esp = [split(x) for x in es]
        inv = [inv[n] - mm3(*tsp[n], *esp[n]) for n in range(count)]
    states = [jnp.concatenate([eyef, jnp.zeros((DK, DV), f32)], axis=1) for _ in range(2)]
    whole = [jnp.ones((1, 1), f32) for _ in range(2)]
    for c in range(chunks):
        b = c * CH
        kqkq, ktkt = shared[c]
        for e in range(2):
            att, gk, gq, tail, dec, br = per[2 * c + e]
            x = states[e]
            u = mm(kqkq, jnp.concatenate(split(x), axis=0))
            uk = u[:CH] * gk
            vcc = vc[b : b + CH, e * DV : (e + 1) * DV].astype(f32)
            r = jnp.concatenate([-uk[:, :DK], vcc - uk[:, DK:]], axis=1)
            fresh = mm3(*split(inv[2 * c + e] * br), *split(r))
            o = u[CH:] * gq + mm(att, jnp.concatenate(split(fresh), axis=0))
            reach[g, b : b + CH, e * DK : (e + 1) * DK] = o[:, :DK].astype(bf16)
            loc[g, b : b + CH, e * DV : (e + 1) * DV] = o[:, DK:]
            whole[e] = whole[e] * dec
            states[e] = x * dec + mm(ktkt, jnp.concatenate(split(fresh * tail), axis=0))
    return states, whole


MAPR = DK + RIM


def prepare(gate, beta, cumc, cumr, betac, betar):
    length = gate.shape[0]
    ii = lax.broadcasted_iota(jnp.int32, (CH, CH), 0)
    jj = lax.broadcasted_iota(jnp.int32, (CH, CH), 1)
    tri = jnp.where(ii >= jj, 1.0, 0.0).astype(bf16)
    pad = jnp.zeros((CH, CH - HV), f32)
    for c in range(length // CH):
        rows = slice(c * CH, (c + 1) * CH)
        x = gate[rows]
        hi, rest = x.astype(bf16), x - x.astype(bf16).astype(f32)
        mid, low = split(rest)
        cum = mm(tri, hi) + mm(tri, mid) + mm(tri, low)
        for val, col, row in ((cum, cumc, cumr), (beta[rows], betac, betar)):
            turned = jnp.concatenate([val, pad], axis=1).T
            for g in range(HK):
                col[g, rows, :] = val[:, 2 * g : 2 * g + 2]
                row[g, :, rows] = turned[2 * g : 2 * g + 2]


def layer_kernel(
    n, doc, q, k, v, wq, wk, wv, gate, beta, z, gain, q_any, k_any, v_any, out,
    rq, rk, rv, cumc, cumr, betac, betar, loc, reach, ext, sbuf, rbuf, ent, inst,
    rim_send, rim_recv, map_send, map_recv, row_send, row_recv, ent_send, ent_recv,
):
    length = q.shape[0]
    t = pl.program_id(0)
    me = lax.axis_index("ctx")
    per_head = n // HV
    rc = DV // per_head
    my_head = me // per_head
    my_row = pl.multiple_of(lax.rem(me, per_head) * rc, rc)

    def remote(src, dst, send, recv, to):
        return pltpu.make_async_remote_copy(
            src_ref=src, dst_ref=dst, send_sem=send, recv_sem=recv,
            device_id={"ctx": to}, device_id_type=pl.DeviceIdType.MESH,
        )

    def rim_copies():
        tail = pl.ds(length - RIM, RIM)
        for i, (a, b) in enumerate(((q_any, rq), (k_any, rk), (v_any, rv))):
            yield remote(a.at[tail], b, rim_send.at[i], rim_recv.at[i], lax.rem(me + 1, n))

    def piece(h, j):
        to = h * per_head + j
        rows = pl.ds(MAPR + j * rc, rc)
        return (
            remote(
                sbuf.at[h, pl.ds(0, MAPR)], rbuf.at[me, pl.ds(0, MAPR)],
                map_send.at[h, j], map_recv.at[me], to,
            ),
            remote(
                sbuf.at[h, rows], rbuf.at[me, pl.ds(MAPR, rc)],
                row_send.at[h, j], row_recv.at[me], to,
            ),
        )

    def arrived(d):
        a, b = pl.ds(0, MAPR), pl.ds(MAPR, rc)
        return (
            remote(sbuf.at[0, a], rbuf.at[d, a], map_send.at[0, 0], map_recv.at[d], d),
            remote(sbuf.at[0, b], rbuf.at[d, b], row_send.at[0, 0], row_recv.at[d], d),
        )

    def entry(d):
        return remote(
            ent.at[d], inst.at[my_head, pl.ds(my_row, rc)], ent_send.at[d], ent_recv.at[me], d
        )

    @pl.when(t == 0)
    def _():
        barrier = pltpu.get_barrier_semaphore()

        def greet(d, _):
            @pl.when(d != me)
            def _():
                pl.semaphore_signal(
                    barrier, inc=1, device_id={"ctx": d}, device_id_type=pl.DeviceIdType.MESH
                )

            return 0

        lax.fori_loop(0, n, greet, 0)
        prepare(gate, beta, cumc, cumr, betac, betar)
        pl.semaphore_wait(barrier, n - 1)

        @pl.when(me < n - 1)
        def _():
            for copy in rim_copies():
                copy.start()

        @pl.when(me == 0)
        def _():
            for r in (rq, rk, rv):
                r[...] = jnp.zeros(r.shape, bf16)

        @pl.when(me > 0)
        def _():
            for copy in rim_copies():
                copy.wait_recv()

        @pl.when(me < n - 1)
        def _():
            for copy in rim_copies():
                copy.wait_send()

    @pl.when(t < HK)
    def _():
        states, whole = slab(
            t, doc, q, k, v, rq, rk, rv, wq, wk, wv, cumc, cumr, betac, betar, loc, reach, ext
        )
        ii = lax.broadcasted_iota(jnp.int32, (DK, DK), 0)
        jj = lax.broadcasted_iota(jnp.int32, (DK, DK), 1)
        ri = lax.broadcasted_iota(jnp.int32, (RIM, DK), 0)
        for e in range(2):
            h = 2 * t + e
            hi = whole[e].astype(bf16).astype(f32)
            mid = (whole[e] - hi).astype(bf16).astype(f32)
            low = whole[e] - hi - mid
            rest = states[e][:, :DK] - jnp.where(ii == jj, whole[e], 0.0)
            facts = jnp.where(ri == 0, hi, jnp.where(ri == 1, mid, jnp.where(ri == 2, low, 0.0)))
            sbuf[h, 0:DK] = rest.astype(bf16)
            sbuf[h, DK:MAPR] = facts.astype(bf16)
            sbuf[h, MAPR : MAPR + DV] = states[e][:, DK:].T.astype(bf16)
            for j in range(per_head):
                @pl.when(h * per_head + j == me)
                def _():
                    rbuf[me, 0:MAPR] = sbuf[h, 0:MAPR]
                    rbuf[me, MAPR : MAPR + rc] = sbuf[h, MAPR + j * rc : MAPR + (j + 1) * rc]

                @pl.when(h * per_head + j != me)
                def _():
                    for copy in piece(h, j):
                        copy.start()

    @pl.when(me // (2 * per_head) == t - LAG)
    def _():
        def step(d, s):
            @pl.when(d != me)
            def _():
                ent[d] = s.astype(bf16)
                entry(d).start()
                for copy in arrived(d):
                    copy.wait_recv()

            @pl.when(d == me)
            def _():
                inst[my_head, pl.ds(my_row, rc)] = s.astype(bf16)

            m = rbuf[d, 0:DK]
            facts = rbuf[d, DK:MAPR].astype(f32)
            decay = jnp.sum(facts, axis=0, keepdims=True)
            moved = mm_nt(jnp.concatenate(split(s), axis=1), jnp.concatenate([m, m], axis=1))
            return s * decay + moved + rbuf[d, MAPR : MAPR + rc].astype(f32)

        lax.fori_loop(0, n, step, jnp.zeros((rc, DK), f32))

    @pl.when(t >= HK)
    def _():
        g = t - HK
        for e in range(2):
            h = 2 * g + e
            for j in range(per_head):
                src = h * per_head + j

                @pl.when(src != me)
                def _():
                    rows = pl.ds(j * rc, rc)
                    remote(
                        ent.at[0], inst.at[h, rows], ent_send.at[0], ent_recv.at[src], src
                    ).wait_recv()

            cols = slice(e * DV, (e + 1) * DV)
            o = loc[g, :, cols] + mm_nt(reach[g, :, cols], inst[h])
            ms = jnp.mean(o * o, axis=-1, keepdims=True)
            zf = z[:, cols].astype(f32)
            gated = o * lax.rsqrt(ms + 1e-6) * gain[...] * (zf / (1.0 + jnp.exp(-zf)))
            out[:, cols] = gated.astype(bf16)

    @pl.when(t == 2 * HK - 1)
    def _():
        def finish(d, _):
            @pl.when(d != me)
            def _():
                entry(d).wait_send()
                for copy in piece(d // per_head, lax.rem(d, per_head)):
                    copy.wait_send()

            return 0

        lax.fori_loop(0, n, finish, 0)


LAG = 2


def local(q_raw, k_raw, v_raw, conv_weight, gate_log, beta, gate_z, norm_gain, doc_start):
    length = q_raw.shape[0]
    taps = conv_weight.shape[0]
    n = lax.axis_size("ctx")
    per_head = n // HV
    rc = DV // per_head
    first = lambda t: jnp.minimum(t, HK - 1)
    second = lambda t: jnp.maximum(t - HK, 0)
    col1 = lambda rows, off=0: pl.BlockSpec((rows, DK), lambda t, off=off: (0, first(t) + off))
    col2 = lambda rows, off=0: pl.BlockSpec((rows, 2 * DV), lambda t, off=off: (0, first(t) + off))
    late = pl.BlockSpec((length, 2 * DV), lambda t: (0, second(t)))
    full = lambda a, b: pl.BlockSpec((a, b), lambda t: (0, 0))
    anywhere = pl.BlockSpec(memory_space=pl.ANY)
    dma = pltpu.SemaphoreType.DMA
    return pl.pallas_call(
        functools.partial(layer_kernel, n),
        grid=(2 * HK,),
        in_specs=[
            pl.BlockSpec(memory_space=pltpu.SMEM),
            col1(length), col1(length), col2(length),
            col1(taps), col1(taps, HK), col2(taps, HK),
            full(length, HV), full(length, HV), late, full(1, DV),
            anywhere, anywhere, anywhere,
        ],
        out_specs=late,
        out_shape=jax.ShapeDtypeStruct((length, HV * DV), bf16),
        scratch_shapes=[
            pltpu.VMEM((RIM, HK * DK), bf16),
            pltpu.VMEM((RIM, HK * DK), bf16),
            pltpu.VMEM((RIM, HV * DV), bf16),
            pltpu.VMEM((HK, length, 2), f32),
            pltpu.VMEM((HK, 2, length), f32),
            pltpu.VMEM((HK, length, 2), f32),
            pltpu.VMEM((HK, 2, length), f32),
            pltpu.VMEM((HK, length, 2 * DV), f32),
            pltpu.VMEM((HK, length, 2 * DK), bf16),
            pltpu.VMEM((length + RIM, 2 * DV), f32),
            pltpu.VMEM((HV, MAPR + DV, DK), bf16),
            pltpu.VMEM((n, MAPR + rc, DK), bf16),
            pltpu.VMEM((n, rc, DK), bf16),
            pltpu.VMEM((HV, DV, DK), bf16),
            dma((3,)), dma((3,)),
            dma((HV, per_head)), dma((n,)),
            dma((HV, per_head)), dma((n,)),
            dma((n,)), dma((n,)),
        ],
        compiler_params=pltpu.CompilerParams(
            vmem_limit_bytes=56 * 1024 * 1024, collective_id=0, has_side_effects=True
        ),
    )(
        doc_start, q_raw, k_raw, v_raw, conv_weight, conv_weight, conv_weight,
        gate_log, beta, gate_z, norm_gain.reshape(1, DV), q_raw, k_raw, v_raw,
    )


def solution(mesh):
    rows = P(("groups", "ctx"), None)
    return jax.shard_map(
        local,
        mesh=mesh,
        in_specs=(rows, rows, rows, P(), rows, rows, rows, P(), P(("groups", "ctx"))),
        out_specs=rows,
        check_vma=False,
    )
```

time: 178 us -> 94.9 us (0.53); the launches traced: 175 us -> 94.4 us
  blocking collectives: 93.1 us -> 0 us
  Pallas kernels: 68.9 us -> 87.4 us
  starting transfers between devices: 3.84 us -> 0 us
  local copies, waits for them, and re-layouts: 8.2 us -> 6.37 us
    all_to_all x3 -> x0, blocking collectives: 93.1 us -> none  [the longest x1 33.8 us: local(): lax.all_to_all(maps_out, 'ctx', split_axis=0, concat_axis=0, tiled=True)]
    pallas_call x3 -> x1, Pallas kernels: 68.9 us -> 87.4 us  [local(): pl.pallas_call(functools.partial(layer_kernel, n), grid=(2 * HK,), in_spe...]
    unnamed x8 -> x3, local copies, waits for them, and re-layouts: 0.02 us -> 6.37 us
    transpose x2 -> x0, local copies, waits for them, and re-layouts: 4 us -> none  [the longest x1 2.02 us: local(): betac, betar = (bet.transpose(1, 0, 2), bet.transpose(1, 2, 0))]
    ppermute x3 -> x0, starting transfers between devices: 3.84 us -> none  [local(): lax.ppermute((q_raw[length - RIM:], k_raw[length - RIM:], v_raw[length -...]
    slice x3 -> x0, local copies, waits for them, and re-layouts: 2.37 us -> none  [the longest x1 0.84 us: local(): v_raw[length - RIM:]]
  transfers between devices with their start and end apart: 3 -> 0, of which waited for: 0 -> 0; matrix products, arithmetic and copies ran while one was open for 4% -> 0% of each run, Pallas kernels for 0% -> 0%
where the time goes in v2:
time: 94.9 us; the launch traced here: 94.4 us
  Pallas kernels  87.4 us (92%)
  local copies, waits for them, and re-layouts  6.37 us (7%)
    pallas_call x1, Pallas kernels, local(): pl.pallas_call(functools.partial(layer_kernel, n), grid=(2 * HK,), in_spe...  87.4 us
    unnamed x3, local copies, waits for them, and re-layouts  6.37 us

profile of v2, /device:TPU:29, one launch (start us, length us, event | category | flops | bytes accessed | tf_op | source)
XLA Modules:
  0.0 94.4 jit_solution(17787441868995200468)
XLA Ops:
  0.7 1.6 %copy.10.gate = f32[512,16]{1,0:T(8,128)} copy(f32[512,16]{0,1:T(8,128)} %param.13) | data formatting | bytes 65536 | tf_op args[4]
  2.2 1.6 %copy.11.beta = f32[512,16]{1,0:T(8,128)} copy(f32[512,16]{0,1:T(8,128)} %param.14) | data formatting | bytes 65536 | tf_op args[5]
  3.9 87.4 %shard_map.91 = bf16[512,2048]{1,0:T(8,128)(2,1)} custom-call(s32[1]{0:T(128)S(6)} %copy.13.doc, bf16[512,1024]{1,0:T(8,128)(2,1)} %q_any.1, bf16[512,1024]{1,0:T(8,128)(2,1)} %k_any.1, bf16[512,2048]{1,0:T(8,128)(2,1)} %v_any.1, f32[4,4096]{1,0:T(4,128)} %wv.1, f32[4,4096]{1,0:T(4,128)} %wv.1, f32[4,4096]{1,0:T(4,128)} %wv.1, f32[512,16]{1,0:T(8,128)} %copy.10.gate, ...), custom_call_target="tpu_custom_call" | custom-call | tf_op jit(solution)/shard_map/pallas_call | solution.py:360
  91.3 3.2 %copy.14 = bf16[512,2048]{1,0:T(8,128)(2,1)} copy(bf16[512,2048]{1,0:T(8,128)(2,1)} %shard_map.91) | data formatting | bytes 4194304

commit v3 on v2

--- a/solution.py
+++ b/solution.py
@@ -28,11 +28,6 @@
 
 def mm_nt(a, b):
     return lax.dot_general(a, b, (((1,), (1,)), ((), ())), preferred_element_type=f32)
-
-
-def mm3(ah, al, bh, bl):
-    left = jnp.concatenate([ah, al], axis=1)
-    return mm(left, jnp.concatenate([bh, bh], axis=0)) + mm(ah, bl)
 
 
 def conv(ext, raw, rim, w, since, length):
@@ -50,7 +45,7 @@
     return (total / (1.0 + jnp.exp(-total))).astype(bf16)
 
 
-def slab(g, doc, q, k, v, rq, rk, rv, wq, wk, wv, cumc, cumr, betac, betar, loc, reach, ext):
+def slab(g, doc, q, k, v, rq, rk, rv, wq, wk, wv, cumc, cumr, betac, loc, reach, ext):
     length = q.shape[0]
     one = pl.multiple_of(g * DK, DK)
     two = pl.multiple_of(g * 2 * DV, 2 * DV)
@@ -94,7 +89,6 @@
             cc = cumc[g, b : b + CH, e : e + 1]
             cr = cumr[g, e : e + 1, b : b + CH]
             bc = betac[g, b : b + CH, e : e + 1]
-            br = betar[g, e : e + 1, b : b + CH]
             decay = jnp.exp(cc - cr + mask)
             lower = gs * decay * bc
             att = ats * decay
@@ -105,49 +99,55 @@
             per.append(
                 (
                     jnp.concatenate([att.astype(bf16)] * 2, axis=1),
-                    growth * k_col,
+                    growth * k_col * bc,
                     growth * q_col,
                     tail,
                     jnp.exp(last) * carries,
-                    br,
+                    bc,
                 )
             )
     count = len(lowers)
     inv = [eyef - jnp.where(ix == 1, lw, 0.0) for lw in lowers]
-    lsp = [split(lw) for lw in lowers]
+    lsp = [lw.astype(bf16) for lw in lowers]
     for lm in range(1, (CH - 1).bit_length()):
         pick = (ix >> lm) == 1
         zero = jnp.zeros((CH, CH), bf16)
-        tsp = [split(t) for t in inv]
-        low = [(jnp.where(pick, a, zero), jnp.where(pick, d, zero)) for a, d in lsp]
-        es = [mm3(*low[n], *tsp[n]) for n in range(count)]
-        esp = [split(x) for x in es]
-        inv = [inv[n] - mm3(*tsp[n], *esp[n]) for n in range(count)]
+        tsp = [m.astype(bf16) for m in inv]
+        low = [jnp.where(pick, a, zero) for a in lsp]
+        es = [mm(low[n], tsp[n]).astype(bf16) for n in range(count)]
+        inv = [inv[n] - mm(tsp[n], es[n]) for n in range(count)]
     states = [jnp.concatenate([eyef, jnp.zeros((DK, DV), f32)], axis=1) for _ in range(2)]
+    tts = [jnp.concatenate([m.astype(bf16)] * 2, axis=1) for m in inv]
     whole = [jnp.ones((1, 1), f32) for _ in range(2)]
     for c in range(chunks):
         b = c * CH
         kqkq, ktkt = shared[c]
-        for e in range(2):
-            att, gk, gq, tail, dec, br = per[2 * c + e]
-            x = states[e]
-            u = mm(kqkq, jnp.concatenate(split(x), axis=0))
-            uk = u[:CH] * gk
-            vcc = vc[b : b + CH, e * DV : (e + 1) * DV].astype(f32)
-            r = jnp.concatenate([-uk[:, :DK], vcc - uk[:, DK:]], axis=1)
-            fresh = mm3(*split(inv[2 * c + e] * br), *split(r))
-            o = u[CH:] * gq + mm(att, jnp.concatenate(split(fresh), axis=0))
+        pair = per[2 * c : 2 * c + 2]
+        us = [mm(kqkq, jnp.concatenate(split(x), axis=0)) for x in states]
+        rs = []
+        for e in range(2):
+            uk = us[e][:CH] * pair[e][1]
+            vcc = vc[b : b + CH, e * DV : (e + 1) * DV].astype(f32) * pair[e][5]
+            rs.append(jnp.concatenate([-uk[:, :DK], vcc - uk[:, DK:]], axis=1))
+        fresh = [
+            mm(tts[2 * c + e], jnp.concatenate(split(rs[e]), axis=0)) for e in range(2)
+        ]
+        for e in range(2):
+            states[e] = states[e] * pair[e][4] + mm(
+                ktkt, jnp.concatenate(split(fresh[e] * pair[e][3]), axis=0)
+            )
+            whole[e] = whole[e] * pair[e][4]
+        for e in range(2):
+            o = us[e][CH:] * pair[e][2] + mm(pair[e][0], jnp.concatenate(split(fresh[e]), axis=0))
             reach[g, b : b + CH, e * DK : (e + 1) * DK] = o[:, :DK].astype(bf16)
             loc[g, b : b + CH, e * DV : (e + 1) * DV] = o[:, DK:]
-            whole[e] = whole[e] * dec
-            states[e] = x * dec + mm(ktkt, jnp.concatenate(split(fresh * tail), axis=0))
     return states, whole
 
 
 MAPR = DK + RIM
 
 
-def prepare(gate, beta, cumc, cumr, betac, betar):
+def prepare(gate, beta, cumc, cumr, betac):
     length = gate.shape[0]
     ii = lax.broadcasted_iota(jnp.int32, (CH, CH), 0)
     jj = lax.broadcasted_iota(jnp.int32, (CH, CH), 1)
@@ -159,16 +159,16 @@
         hi, rest = x.astype(bf16), x - x.astype(bf16).astype(f32)
         mid, low = split(rest)
         cum = mm(tri, hi) + mm(tri, mid) + mm(tri, low)
-        for val, col, row in ((cum, cumc, cumr), (beta[rows], betac, betar)):
-            turned = jnp.concatenate([val, pad], axis=1).T
-            for g in range(HK):
-                col[g, rows, :] = val[:, 2 * g : 2 * g + 2]
-                row[g, :, rows] = turned[2 * g : 2 * g + 2]
+        turned = jnp.concatenate([cum, pad], axis=1).T
+        for g in range(HK):
+            cumc[g, rows, :] = cum[:, 2 * g : 2 * g + 2]
+            cumr[g, :, rows] = turned[2 * g : 2 * g + 2]
+            betac[g, rows, :] = beta[rows, 2 * g : 2 * g + 2]
 
 
 def layer_kernel(
     n, doc, q, k, v, wq, wk, wv, gate, beta, z, gain, q_any, k_any, v_any, out,
-    rq, rk, rv, cumc, cumr, betac, betar, loc, reach, ext, sbuf, rbuf, ent, inst,
+    rq, rk, rv, cumc, cumr, betac, loc, reach, ext, sbuf, rbuf, ent, inst,
     rim_send, rim_recv, map_send, map_recv, row_send, row_recv, ent_send, ent_recv,
 ):
     length = q.shape[0]
@@ -230,7 +230,7 @@
             return 0
 
         lax.fori_loop(0, n, greet, 0)
-        prepare(gate, beta, cumc, cumr, betac, betar)
+        prepare(gate, beta, cumc, cumr, betac)
         pl.semaphore_wait(barrier, n - 1)
 
         @pl.when(me < n - 1)
@@ -256,7 +256,7 @@
     @pl.when(t < HK)
     def _():
         states, whole = slab(
-            t, doc, q, k, v, rq, rk, rv, wq, wk, wv, cumc, cumr, betac, betar, loc, reach, ext
+            t, doc, q, k, v, rq, rk, rv, wq, wk, wv, cumc, cumr, betac, loc, reach, ext
         )
         ii = lax.broadcasted_iota(jnp.int32, (DK, DK), 0)
         jj = lax.broadcasted_iota(jnp.int32, (DK, DK), 1)
@@ -376,7 +376,6 @@
             pltpu.VMEM((HK, length, 2), f32),
             pltpu.VMEM((HK, 2, length), f32),
             pltpu.VMEM((HK, length, 2), f32),
-            pltpu.VMEM((HK, 2, length), f32),
             pltpu.VMEM((HK, length, 2 * DV), f32),
             pltpu.VMEM((HK, length, 2 * DK), bf16),
             pltpu.VMEM((length + RIM, 2 * DV), f32),

time: 94.9 us -> 87.8 us (0.925)
  Pallas kernels: 87.4 us -> 80.3 us
    pallas_call x1, Pallas kernels: 87.4 us -> 80.3 us  [local(): pl.pallas_call(functools.partial(layer_kernel, n), grid=(2 * HK,), in_spe...]
where the time goes in v3:
time: 87.8 us; the launch traced here: 87.3 us
  Pallas kernels  80.3 us (91%)
  local copies, waits for them, and re-layouts  6.37 us (7%)
    pallas_call x1, Pallas kernels, local(): pl.pallas_call(functools.partial(layer_kernel, n), grid=(2 * HK,), in_spe...  80.3 us
    unnamed x3, local copies, waits for them, and re-layouts  6.37 us

profile of v3, /device:TPU:29, one launch (start us, length us, event | category | flops | bytes accessed | tf_op | source)
XLA Modules:
  0.0 87.3 jit_solution(9373485553579584709)
XLA Ops:
  0.7 1.6 %copy.10.gate = f32[512,16]{1,0:T(8,128)} copy(f32[512,16]{0,1:T(8,128)} %param.13) | data formatting | bytes 65536 | tf_op args[4]
  2.2 1.6 %copy.11.beta = f32[512,16]{1,0:T(8,128)} copy(f32[512,16]{0,1:T(8,128)} %param.14) | data formatting | bytes 65536 | tf_op args[5]
  3.9 80.3 %shard_map.91 = bf16[512,2048]{1,0:T(8,128)(2,1)} custom-call(s32[1]{0:T(128)S(6)} %copy.13.doc, bf16[512,1024]{1,0:T(8,128)(2,1)} %q_any.1, bf16[512,1024]{1,0:T(8,128)(2,1)} %k_any.1, bf16[512,2048]{1,0:T(8,128)(2,1)} %v_any.1, f32[4,4096]{1,0:T(4,128)} %wv.1, f32[4,4096]{1,0:T(4,128)} %wv.1, f32[4,4096]{1,0:T(4,128)} %wv.1, f32[512,16]{1,0:T(8,128)} %copy.10.gate, ...), custom_call_target="tpu_custom_call" | custom-call | tf_op jit(solution)/shard_map/pallas_call | solution.py:360
  84.2 3.2 %copy.14 = bf16[512,2048]{1,0:T(8,128)(2,1)} copy(bf16[512,2048]{1,0:T(8,128)(2,1)} %shard_map.91) | data formatting | bytes 4194304
